TPU v7x, 128 devices: a whole 4x4x4 slice. The times are simulated.
128 devices in a mesh: prow: 8 (over x, core), pcol: 16 (over y, z).
Axes of the slice: x: 4, y: 4, z: 4, core: 2. Of those that a mesh axis runs over, the one named last changes fastest.
Arguments:
- samples: float32 [16384, 64], P(('prow', 'pcol'))
- position: int32 [16384], P(('prow', 'pcol')), may hold values from 0 to 16383, as said below
- slot_of_block: int32 [64], replicated, may hold values from 0 to 63, as said below
- structure: int32 [64, 64], replicated, may hold values from 0 to 1, as said below
Outputs:
- panel: float32 [16384, 512], P('prow')
- trailing: float32 [16384, 16384], P('prow', 'pcol')
Inputs may be any that keep to these rules, and one draw needn't show every extreme that they name: A permutation. A sample at position p, in block p div 256 with slot s, is destined for the device at grid row s mod (devices along prow) and grid column (p mod 256) div (256 / devices along pcol). No device holds more than 2 samples for one destination; every device holds exactly 2 for some destination and is the destination of exactly 2 samples from some device; every device is the destination of exactly 128 samples. `slot_of_block`: A permutation. `structure`: Symmetric, with ones on the diagonal.
All inputs are finite; a program needn't handle non-finite values.
Results may differ from a plain program's by a relative error of at most 0.0003.
Values sent between devices are 32-bit elements; how exact they have to be, the bound alone decides.
A program may use at most 128 MiB of HBM per device.

v0:
```python
import math

import jax
import jax.numpy as jnp
from jax import lax
from jax.sharding import PartitionSpec as P

BLOCK = 256


HIGHEST = lax.Precision.HIGHEST
NUGGET = 1.0


def spread(block, axis, source):
    block = jnp.where(lax.axis_index(axis) == source, block, jnp.zeros_like(block))
    return lax.psum(block, axis)


def support_radius(features):
    return 10.0 * math.sqrt(2.0 * features / 3.0)


def kernel_values(left_rows, right_rows, radius):
    left_norm = jnp.sum(left_rows * left_rows, axis=1)[:, None]
    right_norm = jnp.sum(right_rows * right_rows, axis=1)[None, :]
    inner_products = jnp.einsum("af,bf->ab", left_rows, right_rows, precision=HIGHEST)
    squared = jnp.maximum(left_norm + right_norm - 2.0 * inner_products, 0.0)
    scaled = jnp.sqrt(squared) / radius
    remain = jnp.maximum(1.0 - scaled, 0.0)
    return lax.integer_pow(remain, 35) * (35.0 * scaled + 1.0)


def inverse_lower(matrix):
    identity = jnp.eye(matrix.shape[0], dtype=matrix.dtype)
    lower_factor = jnp.linalg.cholesky(matrix)
    inverse = lax.linalg.triangular_solve(lower_factor, identity, left_side=True, lower=True)
    return (lower_factor, inverse)


def place_lower(product, lower_factor, block_ids, block_id):
    product = jnp.where((block_ids == block_id)[:, None, None], lower_factor[None], product)
    return jnp.where((block_ids < block_id)[:, None, None], 0.0, product)


def shards(samples, position, slot_of_block, structure):
    rows_count = lax.axis_size("prow")
    cols_count = lax.axis_size("pcol")
    row_index = lax.axis_index("prow")
    col_index = lax.axis_index("pcol")
    devices = rows_count * cols_count
    local_count, features = samples.shape
    blocks_total = slot_of_block.shape[0]
    row_blocks = blocks_total // rows_count
    col_blocks = blocks_total // cols_count
    row_share = BLOCK // cols_count
    capacity = max(2, 2 * local_count // devices)
    radius = support_radius(features)
    block_order = jnp.arange(blocks_total, dtype=jnp.int32)
    matches = slot_of_block[None, :] == block_order[:, None]
    block_at_slot = jnp.sum(jnp.where(matches, block_order[None, :], 0), axis=1)

    def slot_lookup(block_ids):
        return jnp.sum(
            jnp.where(block_ids[:, None] == block_order[None, :], slot_of_block[None, :], 0), axis=1
        )

    def block_lookup(slot_values):
        return jnp.sum(
            jnp.where(slot_values[:, None] == block_order[None, :], block_at_slot[None, :], 0),
            axis=1,
        )

    slot_values = slot_lookup(position // BLOCK)
    target = slot_values % rows_count * cols_count + position % BLOCK // row_share
    onehot = (target[:, None] == jnp.arange(devices, dtype=jnp.int32)[None, :]).astype(jnp.int32)
    rank_within = jnp.sum(onehot * (jnp.cumsum(onehot, axis=0) - 1), axis=1)
    bucket = target * capacity + rank_within
    send_points = jnp.zeros((devices * capacity, features), jnp.float32).at[bucket].set(samples)
    send_places = jnp.full((devices * capacity,), -1, jnp.int32).at[bucket].set(position)
    got_points, got_places = (
        lax.all_to_all(
            send_points.reshape(devices, capacity * features),
            ("prow", "pcol"),
            split_axis=0,
            concat_axis=0,
            tiled=True,
        ),
        lax.all_to_all(
            send_places.reshape(devices, capacity),
            ("prow", "pcol"),
            split_axis=0,
            concat_axis=0,
            tiled=True,
        ),
    )
    got_points = got_points.reshape(devices * capacity, features)
    got_places = got_places.reshape(devices * capacity)
    valid_places = jnp.maximum(got_places, 0)
    got_slots = slot_lookup(valid_places // BLOCK)
    local_row = got_slots // rows_count * row_share + valid_places % BLOCK % row_share
    local_row = jnp.where(got_places >= 0, local_row, row_blocks * row_share)
    local_rows = (
        jnp.zeros((row_blocks * row_share, features), jnp.float32)
        .at[local_row]
        .set(got_points, mode="drop")
    )
    row_points = lax.all_gather(
        local_rows.reshape(row_blocks, row_share * features), "pcol", axis=1, tiled=True
    )
    row_points = row_points.reshape(row_blocks, BLOCK, features)
    picked = lax.dynamic_index_in_dim(
        row_points.reshape(col_blocks, cols_count // rows_count, BLOCK * features),
        col_index // rows_count,
        1,
        keepdims=False,
    )
    col_points = spread(picked, "prow", col_index % rows_count).reshape(col_blocks, BLOCK, features)
    row_ids = block_lookup(jnp.arange(row_blocks, dtype=jnp.int32) * rows_count + row_index)
    col_ids = block_lookup(jnp.arange(col_blocks, dtype=jnp.int32) * cols_count + col_index)
    weights = structure.astype(jnp.float32)
    onehot_rows = (row_ids[:, None] == block_order[None, :]).astype(jnp.float32)
    onehot_cols = (col_ids[:, None] == block_order[None, :]).astype(jnp.float32)
    local_weights = jnp.dot(jnp.dot(onehot_rows, weights), onehot_cols.T)
    identity = jnp.eye(BLOCK, dtype=jnp.float32)
    values = kernel_values(
        row_points.reshape(-1, features), col_points.reshape(-1, features), radius
    )
    values = values.reshape(row_blocks, BLOCK, col_blocks, BLOCK) * local_weights[:, None, :, None]
    same_block = (row_ids[:, None] == col_ids[None, :]).astype(jnp.float32)
    values = values + NUGGET * same_block[:, None, :, None] * identity[None, :, None, :]

    def factor_owner(column, block_id):
        slot_value = slot_of_block[block_id]
        root_row = slot_value % rows_count
        root_col = slot_value % cols_count
        is_owner = (row_index == root_row) & (col_index == root_col)
        diagonal = lax.dynamic_index_in_dim(column, slot_value // rows_count, 0, keepdims=False)
        lower_factor, inverse = inverse_lower(jnp.where(is_owner, diagonal, identity))
        lower_factor, inverse = (
            spread(lower_factor, "prow", root_row),
            spread(inverse, "prow", root_row),
        )
        product = jnp.einsum("kab,cb->kac", column, inverse, precision=HIGHEST)
        product = place_lower(product, lower_factor, row_ids, block_id)
        rows_part = spread(product, "pcol", root_col)
        chosen = lax.dynamic_index_in_dim(
            rows_part.reshape(col_blocks, cols_count // rows_count, BLOCK, BLOCK),
            col_index // rows_count,
            1,
            keepdims=False,
        )
        cols_part = spread(chosen, "prow", col_index % rows_count)
        return (rows_part, cols_part)

    slot_first = slot_of_block[0]
    slot_second = slot_of_block[1]
    column_first = lax.dynamic_index_in_dim(values, slot_first // cols_count, 2, keepdims=False)
    rows_first, cols_first = factor_owner(column_first, 0)
    column_second = lax.dynamic_index_in_dim(values, slot_second // cols_count, 2, keepdims=False)
    link_block = lax.dynamic_index_in_dim(cols_first, slot_second // cols_count, 0, keepdims=False)
    column_second = column_second - jnp.einsum(
        "kab,cb->kac", rows_first, link_block, precision=HIGHEST
    )
    rows_second, cols_second = factor_owner(column_second, 1)
    result = values - jnp.einsum("kac,mbc->kamb", rows_first, cols_first, precision=HIGHEST)
    result = result - jnp.einsum("kac,mbc->kamb", rows_second, cols_second, precision=HIGHEST)
    kept_mask = (col_ids[None, :] <= row_ids[:, None]) & (col_ids[None, :] >= 2)
    result = jnp.where(kept_mask[:, None, :, None], result, 0.0)
    trailing = result.reshape(row_blocks * BLOCK, col_blocks * BLOCK)
    panel_out = jnp.concatenate([rows_first, rows_second], axis=-1).reshape(
        row_blocks * BLOCK, 2 * BLOCK
    )
    return (panel_out, trailing)


def solution(mesh):
    in_specs = (P(("prow", "pcol"), None), P(("prow", "pcol")), P(), P())
    out_specs = (P("prow", None), P("prow", "pcol"))
    return jax.shard_map(shards, mesh=mesh, in_specs=in_specs, out_specs=out_specs, check_vma=False)
```

profile of v0, /device:TPU:8, one launch (start us, length us, event | category | flops | bytes accessed | tf_op | source)
XLA Modules:
  0.0 785.2 jit_solution(5070634052825868046)
XLA Ops:
  11.6 10.4 %all-to-all-start = ((s32[128,1,2]{2,1,0:T(1,128)}), s32[128,1,2]{2,1,0:T(1,128)S(1)}, u32[]{:S(2)}, u32[]{:S(2)}) async-start(s32[128,1,2]{2,1,0:T(1,128)} %bitcast.1), calls=%async_computation | async-start | bytes 131072 | tf_op jit(solution)/shard_map/all_to_all | solution.py:89
  31.1 9.7 %all-to-all-start.1 = ((f32[128,1,128]{2,1,0:T(1,128)}), f32[128,1,128]{2,1,0:T(1,128)S(1)}, u32[]{:S(2)}, u32[]{:S(2)}) async-start(f32[128,1,128]{2,1,0:T(1,128)} %bitcast.4), calls=%async_computation.1 | async-start | bytes 131072 | tf_op jit(solution)/shard_map/all_to_all | solution.py:82
  43.2 6.7 all-to-all-done.1
  52.6 22.3 %all_gather.3 = f32[8,16384]{1,0:T(8,128)S(1)} all-gather(f32[8,1024]{1,0:T(8,128)S(1)} %reshape.336), channel_id=1, replica_groups=mesh['prow'=8,'pcol'=16] {'pcol'}, dimensions={1}, use_global_device_ids=true | all-gather | bytes 557056 | tf_op jit(solution)/shard_map/all_gather | solution.py:108
  77.9 57.4 %all-reduce.11.cloned.1.call-done = f32[1024,64]{1,0:T(8,128)} async-done(((f32[1024,64]{1,0:T(8,128)}), f32[1024,64]{1,0:T(8,128)}) %all-reduce.11.cloned.1.call-update) | async-done | bytes 262160 | tf_op jit(solution)/shard_map/psum | solution.py:17
  136.6 16.1 %fusion.1 = f32[2048,1024]{1,0:T(8,128)} fusion(f32[2048,64]{1,0:T(8,128)S(1)} %reshape_reshape.9, f32[1024,64]{1,0:T(8,128)} %all-reduce.11.cloned.1.call-done, f32[1024]{0:T(1024)S(1)} %multiply_reduce_fusion.1, f32[2048]{0:T(1024)S(1)} %multiply_reduce_fusion), kind=kOutput, calls=%fused_computation.10 | convolution fusion | flops 1646264320 | bytes 9187328 | tf_op jit(solution)/shard_map/af,bf->ab/dot_general | solution.py:27
  152.7 11.1 %reshape.337 = f32[8,256,4,256]{3,2,1,0:T(4,128)} reshape(f32[2048,1024]{1,0:T(8,128)} %fusion.1) | data formatting | bytes 16777216 | tf_op jit(solution)/shard_map/reshape | solution.py:129
  163.8 5.5 fusion.5
  169.3 3.4 copy-done
  173.1 11.7 %cholesky.130 = f32[128,128]{1,0:T(8,128)S(1)} custom-call(f32[128,128]{1,0:T(8,128)S(1)} %cholesky.194), custom_call_target="Cholesky" | custom-call | tf_op jit(solution)/shard_map/jit(cholesky)/cholesky | solution.py:36
  184.8 9.8 %custom-call.13 = f32[1,128,128]{1,2,0:T(8,128)S(1)} custom-call(f32[1,128,128]{2,1,0:T(8,128)S(1)} %get-tuple-element.65), custom_call_target="InvertDiagBlocksLowerTriangular" | custom-call | tf_op jit(solution)/shard_map/jit(cholesky)/cholesky | solution.py:36
  195.1 11.9 %cholesky.147 = f32[128,128]{1,0:T(8,128)S(1)} custom-call(f32[128,128]{1,0:T(8,128)S(1)} %convolution_subtract_fusion.3), custom_call_target="Cholesky" | custom-call | tf_op jit(solution)/shard_map/jit(cholesky)/cholesky | solution.py:36
  209.9 4.1 while.4
  214.0 19.7 %custom-call.14 = f32[2,128,128]{1,2,0:T(8,128)S(1)} custom-call(f32[2,128,128]{2,1,0:T(8,128)S(1)} %get-tuple-element.18), custom_call_target="InvertDiagBlocksLowerTriangular" | custom-call | tf_op jit(solution)/shard_map/triangular_solve/custom-call.0 | solution.py:37
  235.5 60.1 %all-reduce.23.cloned.1.call-done = (f32[256,256]{1,0:T(8,128)}, f32[256,256]{1,0:T(8,128)}) async-done(((f32[256,256]{1,0:T(8,128)}, f32[256,256]{1,0:T(8,128)}), (f32[256,256]{1,0:T(8,128)}, f32[256,256]{1,0:T(8,128)})) %all-reduce.23.cloned.1.call-update) | async-done | bytes 524304 | tf_op jit(solution)/shard_map/psum | solution.py:17
  295.7 4.8 select_select_fusion.1
  300.6 89.5 %all-reduce.13.cloned.1.call-done = f32[8,256,256]{2,1,0:T(8,128)} async-done(((f32[8,256,256]{2,1,0:T(8,128)}), f32[8,256,256]{2,1,0:T(8,128)}) %all-reduce.13.cloned.1.call-update) | async-done | bytes 2097168 | tf_op jit(solution)/shard_map/psum | solution.py:17
  395.0 59.9 %all-reduce.15.cloned.1.call-done = f32[4,256,256]{2,1,0:T(8,128)} async-done(((f32[4,256,256]{2,1,0:T(8,128)}), f32[4,256,256]{2,1,0:T(8,128)}) %all-reduce.15.cloned.1.call-update) | async-done | bytes 1048592 | tf_op jit(solution)/shard_map/psum | solution.py:17
  454.9 4.3 bitcast_subtract_fusion
  461.0 11.7 %cholesky.164 = f32[128,128]{1,0:T(8,128)S(1)} custom-call(f32[128,128]{1,0:T(8,128)S(1)} %cholesky.197), custom_call_target="Cholesky" | custom-call | tf_op jit(solution)/shard_map/jit(cholesky)/cholesky | solution.py:36
  472.7 9.8 %custom-call.15 = f32[1,128,128]{1,2,0:T(8,128)S(1)} custom-call(f32[1,128,128]{2,1,0:T(8,128)S(1)} %get-tuple-element.61), custom_call_target="InvertDiagBlocksLowerTriangular" | custom-call | tf_op jit(solution)/shard_map/jit(cholesky)/cholesky | solution.py:36
  483.0 12.1 %cholesky.181 = f32[128,128]{1,0:T(8,128)S(1)} custom-call(f32[128,128]{1,0:T(8,128)S(1)} %convolution_subtract_fusion.2), custom_call_target="Cholesky" | custom-call | tf_op jit(solution)/shard_map/jit(cholesky)/cholesky | solution.py:36
  498.5 3.8 while.5
  502.3 19.7 %custom-call.16 = f32[2,128,128]{1,2,0:T(8,128)S(1)} custom-call(f32[2,128,128]{2,1,0:T(8,128)S(1)} %get-tuple-element.19), custom_call_target="InvertDiagBlocksLowerTriangular" | custom-call | tf_op jit(solution)/shard_map/triangular_solve/custom-call.0 | solution.py:37
  523.8 60.2 %all-reduce.21.cloned.1.call-done = (f32[256,256]{1,0:T(8,128)}, f32[256,256]{1,0:T(8,128)}) async-done(((f32[256,256]{1,0:T(8,128)}, f32[256,256]{1,0:T(8,128)}), (f32[256,256]{1,0:T(8,128)}, f32[256,256]{1,0:T(8,128)})) %all-reduce.21.cloned.1.call-update) | async-done | bytes 524304 | tf_op jit(solution)/shard_map/psum | solution.py:17
  583.9 4.8 select_select_fusion
  588.8 89.5 %all-reduce.17.cloned.1.call-done = f32[8,256,256]{2,1,0:T(8,128)} async-done(((f32[8,256,256]{2,1,0:T(8,128)}), f32[8,256,256]{2,1,0:T(8,128)}) %all-reduce.17.cloned.1.call-update) | async-done | bytes 2097168 | tf_op jit(solution)/shard_map/psum | solution.py:17
  680.7 9.0 %fusion.7 = f32[8,256,4,256]{3,1,2,0:T(8,128)} fusion(f32[8,256,256]{2,1,0:T(8,128)S(1)} %copy-done.1, f32[4,256,256]{2,1,0:T(8,128)S(1)} %copy-done.4), kind=kOutput, calls=%fused_computation.19 | convolution fusion | flops 6442450944 | bytes 11534336 | tf_op jit(solution)/shard_map/kac,mbc->kamb/dot_general | solution.py:166
  692.2 50.5 %all-reduce.19.cloned.1.call-done = f32[4,256,256]{2,1,0:T(8,128)} async-done(((f32[4,256,256]{2,1,0:T(8,128)}), f32[4,256,256]{2,1,0:T(8,128)}) %all-reduce.19.cloned.1.call-update) | async-done | bytes 1048592 | tf_op jit(solution)/shard_map/psum | solution.py:17
  742.7 14.6 %subtract_select_fusion = f32[8,256,4,256]{3,1,2,0:T(8,128)} fusion(f32[8,256,4,256]{3,1,2,0:T(8,128)} %copy-done, f32[8,256,4,256]{3,1,2,0:T(8,128)} %fusion.7, pred[8,4]{1,0:T(8,128)(4,1)S(1)} %get-tuple-element.66, f32[8,256,256]{2,1,0:T(8,128)} %all-reduce.17.cloned.1.call-done, f32[4,256,256]{2,1,0:T(8,128)} %all-reduce.19.cloned.1.call-done), kind=kOutput, calls=%fused_computation.16 | convolution fusion | flops 6448742400 | bytes 28311584 | tf_op jit(solution)/shard_map/kac,mbc->kamb/dot_general | solution.py:167
  757.3 12.0 %copy.67 = f32[8,256,4,256]{3,2,1,0:T(4,128)} copy(f32[8,256,4,256]{3,1,2,0:T(8,128)} %subtract_select_fusion) | data formatting | bytes 16777216
  769.3 8.9 %copy.72 = f32[256,8,4,256]{3,1,2,0:T(8,128)} copy(f32[256,8,4,256]{3,2,1,0:T(4,128)} %bitcast.133) | data formatting | bytes 16777216
  (123 shorter events, 45.4 us)
Async XLA Ops:
  11.6 19.5 %all-to-all-start = ((s32[128,1,2]{2,1,0:T(1,128)}), s32[128,1,2]{2,1,0:T(1,128)S(1)}, u32[]{:S(2)}, u32[]{:S(2)}) async-start(s32[128,1,2]{2,1,0:T(1,128)} %bitcast.1), calls=%async_computation | async-start | bytes 131072 | tf_op jit(solution)/shard_map/all_to_all | solution.py:89
  31.1 18.8 %all-to-all-start.1 = ((f32[128,1,128]{2,1,0:T(1,128)}), f32[128,1,128]{2,1,0:T(1,128)S(1)}, u32[]{:S(2)}, u32[]{:S(2)}) async-start(f32[128,1,128]{2,1,0:T(1,128)} %bitcast.4), calls=%async_computation.1 | async-start | bytes 131072 | tf_op jit(solution)/shard_map/all_to_all | solution.py:82
  40.8 94.5 %all-reduce.11.cloned.1.call-start = ((), (), s32[]{:S(2)}) async-start(), calls=%async_computation.2 | async-start | bytes 1048576 | tf_op jit(solution)/shard_map/psum | solution.py:17
  77.3 218.4 %all-reduce.23.cloned.1.call-start = ((), (), s32[]{:S(2)}) async-start(), calls=%async_computation.8 | async-start | bytes 1048576 | tf_op jit(solution)/shard_map/psum | solution.py:17
  169.3 3.4 copy-start
  235.5 154.6 %all-reduce.13.cloned.1.call-start = ((), (), s32[]{:S(2)}) async-start(), calls=%async_computation.3 | async-start | bytes 4194304 | tf_op jit(solution)/shard_map/psum | solution.py:17
  300.5 154.4 %all-reduce.15.cloned.1.call-start = ((), (), s32[]{:S(2)}) async-start(), calls=%async_computation.4 | async-start | bytes 2097152 | tf_op jit(solution)/shard_map/psum | solution.py:17
  392.4 191.5 %all-reduce.21.cloned.1.call-start = ((), (), s32[]{:S(2)}) async-start(), calls=%async_computation.7 | async-start | bytes 1048576 | tf_op jit(solution)/shard_map/psum | solution.py:17
  459.2 1.3 copy-start.3
  460.7 219.9 %copy-start.1 = (f32[8,256,256]{2,1,0:T(8,128)S(1)}, f32[8,256,256]{2,1,0:T(8,128)}, u32[]{:S(2)}) copy-start(f32[8,256,256]{2,1,0:T(8,128)} %all-reduce.13.cloned.1.call-done) | copy-start | bytes 6291460
  522.7 158.0 %copy-start.4 = (f32[4,256,256]{2,1,0:T(8,128)S(1)}, f32[4,256,256]{2,1,0:T(8,128)}, u32[]{:S(2)}) copy-start(f32[4,256,256]{2,1,0:T(8,128)} %all-reduce.15.cloned.1.call-done) | copy-start | bytes 3145732
  523.7 154.6 %all-reduce.17.cloned.1.call-start = ((), (), s32[]{:S(2)}) async-start(), calls=%async_computation.5 | async-start | bytes 4194304 | tf_op jit(solution)/shard_map/psum | solution.py:17
  588.8 153.9 %all-reduce.19.cloned.1.call-start = ((), (), s32[]{:S(2)}) async-start(), calls=%async_computation.6 | async-start | bytes 2097152 | tf_op jit(solution)/shard_map/psum | solution.py:17
  680.6 9.0 %copy-start.2 = (f32[8,256,256]{2,1,0:T(8,128)S(1)}, f32[8,256,256]{2,1,0:T(8,128)}, u32[]{:S(2)}) copy-start(f32[8,256,256]{2,1,0:T(8,128)} %all-reduce.17.cloned.1.call-done) | copy-start | bytes 6291460
Sparse Core Ops, SparseCore 0:
  77.4 57.9 all-reduce.10
  235.6 60.0 all-reduce.22
  300.6 89.4 all-reduce.12
  393.0 61.8 all-reduce.14
  523.9 60.0 all-reduce.20
  588.9 89.3 all-reduce.16
  680.8 61.8 all-reduce.18
where the time goes:
time: 792 us; the launch traced here: 785 us
  waiting for transfers between devices  474 us (60%)
  other arithmetic  132 us (17%)
  matrix products  57.6 us (7%)
  local copies, waits for them, and re-layouts  55.4 us (7%)
  between operations  22.7 us (3%)
  blocking collectives  22.3 us (3%)
  starting transfers between devices  20.7 us (3%)
    psum x7, waiting for transfers between devices, spread(): return lax.psum(block, axis)  467 us
    another operation x13, other arithmetic, inverse_lower(): lower_factor = jnp.linalg.cholesky(matrix)  69.2 us
    another operation x5, other arithmetic, inverse_lower(): lax.linalg.triangular_solve(lower_factor, identity, left_side=True, lower...  40.9 us
    unnamed x13, local copies, waits for them, and re-layouts  26.4 us
    all_gather x1, blocking collectives, shards(): lax.all_gather(local_rows.reshape(row_blocks, row_share * features), 'pco...  22.3 us
    dot_general x1, matrix products, kernel_values(): jnp.einsum('af,bf->ab', left_rows, right_rows, precision=HIGHEST)  16.1 us
  transfers between devices with their start and end apart: 9, of which 9 were waited for; matrix products, arithmetic and copies ran while one was open for 3% of the time, Pallas kernels for 0%

commit v1 on v0

v1 whole, which is shorter than its diff:
```python
import functools
import math

import jax
import jax.numpy as jnp
from jax import lax
from jax.experimental import pallas as pl
from jax.experimental.pallas import tpu as pltpu
from jax.sharding import PartitionSpec as P

BLOCK = 256
FEAT = 64
NBLK = 64
NR = 8
NC = 16
SRC = 128
SHARE = BLOCK // NC
ROWB = NBLK // NR
COLB = NBLK // NC
RADIUS = 10.0 * math.sqrt(2.0 * FEAT / 3.0)
F32 = jnp.float32
BF16 = jnp.bfloat16
I32 = jnp.int32
STEP = 64
HOP1 = 3 * NC + 8
NUGGET = 1.0
VMEM_LIMIT = 58 * 1024 * 1024
HIGHEST = lax.Precision.HIGHEST
MESH = pl.DeviceIdType.MESH
NT = (((1,), (1,)), ((), ()))
NN = (((1,), (0,)), ((), ()))


def iota(shape, axis):
    return lax.broadcasted_iota(I32, shape, axis)


def mm(a, b, dims=NN, precision=None):
    return lax.dot_general(a, b, dims, precision=precision, preferred_element_type=F32)


def pieces(x):
    h = x.astype(BF16)
    left = x - h.astype(F32)
    m = left.astype(BF16)
    return [h, m, (left - m.astype(F32)).astype(BF16)]


def exchange_kernel(
    samples_ref, position_ref, slot_ref, structure_ref,
    rows_ref, cols_ref, diag_ref, x0_ref, x1_ref, l_ref,
    buf1, recv1, buf2, recv2, chunk, dshare, cols_a, cols_l, inverses, whole, scratch, below_l, below_r,
    s1, r1, s2, r2, s4, r4, s5, r5, s6, r6, own,
):
    r = lax.axis_index("prow")
    c = lax.axis_index("pcol")
    source_row = lax.rem(c, NR)
    barrier = pltpu.get_barrier_semaphore()

    def greet(row, col):
        pl.semaphore_signal(barrier, inc=1, device_id=(row, col), device_id_type=MESH)

    for d in range(1, NR):
        greet(lax.rem(r + d, NR), c)
    for d in range(1, NC):
        greet(r, lax.rem(c + d, NC))

    place = position_ref[...]
    block = place >> 8
    share = (place & 255) >> 4
    in_block = (iota((NBLK, SRC), 0) == block).astype(F32)
    slots_row = jnp.broadcast_to(slot_ref[...].astype(F32), (8, NBLK))
    slot = mm(slots_row, in_block)[0:1].astype(I32)
    dest_row = slot & (NR - 1)
    row_in_share = (place & (SHARE - 1)) + 1
    earlier = (iota((SRC, SRC), 0) < iota((SRC, SRC), 1)).astype(F32)

    def buckets(count, target):
        hit = (iota((count, SRC), 0) == target).astype(F32)
        before = mm(hit, earlier)
        rank = jnp.sum(hit * before, axis=0, keepdims=True).astype(I32)
        return hit * (rank == 0).astype(F32), hit * (rank == 1).astype(F32), rank

    first, second, rank = buckets(SRC, dest_row * NC + share)
    leading = block < 2
    pair = jnp.where(leading, share * 2 + block, -1)
    first01, second01, rank01 = buckets(2 * NC, pair)
    doubled = pieces(jnp.concatenate([samples_ref[...], samples_ref[...]], axis=0))
    low128 = iota((SRC, SRC), 1) < FEAT
    onehot = jnp.concatenate([first, first01, second, second01], axis=0).astype(BF16)
    picked = mm(
        jnp.concatenate([onehot] * 3, axis=1), jnp.concatenate(doubled, axis=1), NT
    )
    half = SRC + 2 * NC
    data = jnp.where(iota((half, SRC), 1) < FEAT, picked[:half], picked[half:])
    to_row = (iota((NR, SRC), 0) == dest_row).astype(F32)
    lanes = iota((SRC, SRC), 0)
    tags = (lanes == share * 2 + rank).astype(F32) * ((slot >> 3) * SHARE + row_in_share).astype(F32)
    lane01 = jnp.where(leading, 2 * NC + pair * 2 + rank01, -1)
    tags01 = (lanes == lane01).astype(F32) * row_in_share.astype(F32)
    meta = mm(
        jnp.concatenate([to_row, jnp.ones((NR, SRC), F32)], axis=1),
        jnp.concatenate([tags, tags01], axis=1),
        NT,
    )
    for i in range(NR):
        buf1[i, 0:NC] = data[i * NC : (i + 1) * NC]
        buf1[i, NC : 3 * NC] = data[SRC:]
        buf1[i, 3 * NC : 3 * NC + 8] = jnp.broadcast_to(meta[i : i + 1], (8, SRC))

    pl.semaphore_wait(barrier, (NR - 1) + (NC - 1))

    first_hop = []
    for d in range(1, NR):
        to = lax.rem(r + d, NR)
        copy = pltpu.make_async_remote_copy(
            buf1.at[to], recv1.at[pl.ds(HOP1 * d, HOP1)], s1.at[d], r1.at[d],
            device_id=(to, c), device_id_type=MESH,
        )
        copy.start()
        first_hop.append(copy)
    recv1[0:HOP1] = buf1[r]
    for copy in first_hop:
        copy.wait_recv()

    def every(row):
        return recv1[pl.ds(row, NR, stride=HOP1), :]

    tag_rows = every(3 * NC)
    for q in range(NC):
        buf2[q, 0:8] = every(q)
        buf2[q, 8:16] = every(NC + 2 * q)
        buf2[q, 16:24] = every(NC + 2 * q + 1)
        buf2[q, 24:32] = tag_rows
    second_hop = []
    for d in range(1, NC):
        to = lax.rem(c + d, NC)
        copy = pltpu.make_async_remote_copy(
            buf2.at[to], recv2.at[d], s2.at[d], r2.at[d], device_id=(r, to), device_id_type=MESH
        )
        copy.start()
        second_hop.append(copy)
    recv2[0] = buf2[c]
    for copy in second_hop:
        copy.wait_recv()

    line = iota((8, SRC), 0)
    mine = jnp.where(line < 2, 2 * c + line, 2 * NC + 4 * c + line - 2)
    mine = (iota((8, SRC), 1) == mine) & (line < 6)
    tag = mm(mine.astype(F32), recv2[:, 24:32, :].reshape(SRC, SRC), NT).astype(I32)

    def settle(count, part, line):
        got = recv2[:, 8 * part : 8 * part + 8, :].reshape(SRC, SRC)
        turned = pltpu.roll(got, FEAT, 1)
        both = jnp.concatenate(
            [jnp.where(low128, got, turned), jnp.where(low128, turned, got)], axis=0
        )
        wanted = jnp.concatenate([tag[line : line + 1], tag[line + 1 : line + 2]], axis=1)
        onehot = (iota((count, 2 * SRC), 0) + 1 == wanted).astype(F32).astype(BF16)
        return mm(
            jnp.concatenate([onehot] * 3, axis=1), jnp.concatenate(pieces(both), axis=0), NN
        )

    low16 = iota((SHARE, SRC), 1) < FEAT
    dshare[...] = jnp.where(low16, settle(SHARE, 1, 2), settle(SHARE, 2, 4))
    my_rows = pl.ds(pl.multiple_of(c * SHARE, SHARE), SHARE)
    diag_copies = []
    for d in range(1, NC):
        copy = pltpu.make_async_remote_copy(
            dshare, diag_ref.at[my_rows, :], s6.at[d], r6.at[c],
            device_id=(r, lax.rem(c + d, NC)), device_id_type=MESH,
        )
        copy.start()
        diag_copies.append(copy)
    diag_ref[my_rows, :] = dshare[...]

    placed = settle(SRC, 0, 0)
    low64 = iota((64, SRC), 1) < FEAT
    chunk[...] = jnp.where(low64, placed[0:64], placed[64:128]).reshape(2, 2, SHARE, SRC)
    row_copies = []
    for d in range(1, NC):
        copy = pltpu.make_async_remote_copy(
            chunk, rows_ref.at[:, :, my_rows, :], s4.at[d], r4.at[c],
            device_id=(r, lax.rem(c + d, NC)), device_id_type=MESH,
        )
        copy.start()
        row_copies.append(copy)
    own_rows = pltpu.make_async_copy(chunk, rows_ref.at[:, :, my_rows, :], own.at[0])
    own_rows.start()

    def from_device(d):
        q = lax.rem(c + d, NC)
        return q, pl.ds(pl.multiple_of(q * SHARE, SHARE), SHARE)

    cols_a[...] = jnp.zeros_like(cols_a)
    cols_l[...] = jnp.zeros_like(cols_l)
    whole[...] = jnp.zeros_like(whole)
    below_l[...] = jnp.zeros_like(below_l)
    below_r[...] = jnp.zeros_like(below_r)
    for copy in first_hop + second_hop:
        copy.wait_send()
    for d in range(1, NC):
        q, spot = from_device(d)
        pltpu.make_async_copy(dshare, diag_ref.at[spot, :], r6.at[q]).wait()

    left0, right0 = point_operands(diag_ref[...], 0)
    left1, right1 = point_operands(diag_ref[...], 1)
    weight = structure_ref[1, 0].astype(F32)
    for i, j, left, right in ((0, 0, left0, right0), (1, 0, left1, right0), (1, 1, left1, right1)):
        l_ref[0:BLOCK, 0:BLOCK] = mm(left, right, NT)
        for s in range(0, BLOCK, STEP):
            value = kappa(l_ref[s : s + STEP, 0:BLOCK])
            if i == j:
                on = iota((STEP, BLOCK), 0) + s == iota((STEP, BLOCK), 1)
                value = jnp.where(on, value + NUGGET, value)
            else:
                value = value * weight
            for g in range(BLOCK // STEP):
                cols_a[j * (BLOCK // STEP) + g, i * BLOCK + s : i * BLOCK + s + STEP, :] = value[
                    :, g * STEP : (g + 1) * STEP
                ]

    col_half = lax.div(c, NR)

    def col_copy(d):
        return pltpu.make_async_remote_copy(
            rows_ref.at[:, col_half], cols_ref, s5.at[d], r5.at[0],
            device_id=(lax.rem(r + d, NR), c), device_id_type=MESH,
        )

    own_cols = pltpu.make_async_copy(rows_ref.at[:, col_half], cols_ref, own.at[1])

    def pass_columns():
        for d in range(1, NC):
            q, spot = from_device(d)
            pltpu.make_async_copy(chunk, rows_ref.at[:, :, spot, :], r4.at[q]).wait()
        own_rows.wait()

        @pl.when(source_row == r)
        def _():
            for d in range(1, NR):
                col_copy(d).start()
            own_cols.start()

    factor(cols_a, cols_l, inverses, whole, l_ref, scratch, below_l, below_r, pass_columns)
    high, rest = halves(whole[...])
    for x_ref, top, count in ((x0_ref, 0, 1), (x1_ref, BLOCK, 2)):
        for b in range(count):
            spot = (slice(top, top + BLOCK), slice(BLOCK * b, BLOCK * (b + 1)))
            base = 3 * BLOCK * b
            x_ref[:, base : base + BLOCK] = high[spot]
            x_ref[:, base + BLOCK : base + 2 * BLOCK] = high[spot]
            x_ref[:, base + 2 * BLOCK : base + 3 * BLOCK] = rest[spot]

    @pl.when(source_row == r)
    def _():
        for d in range(1, NR):
            col_copy(d).wait_send()
        own_cols.wait()

    @pl.when(source_row != r)
    def _():
        pltpu.make_async_copy(rows_ref.at[:, 0], cols_ref, r5.at[0]).wait()

    for copy in row_copies + diag_copies:
        copy.wait_send()


def exchange(samples, position, slots, structure):
    dma = pltpu.SemaphoreType.DMA
    vmem = pl.BlockSpec(memory_space=pltpu.VMEM)
    smem = pl.BlockSpec(memory_space=pltpu.SMEM)
    hbm = pl.BlockSpec(memory_space=pl.ANY)
    n2 = 2 * BLOCK
    steps = n2 // STEP
    return pl.pallas_call(
        exchange_kernel,
        out_shape=(
            jax.ShapeDtypeStruct((2, 2, BLOCK, 128), F32),
            jax.ShapeDtypeStruct((2, BLOCK, 128), F32),
            jax.ShapeDtypeStruct((BLOCK, 128), F32),
            jax.ShapeDtypeStruct((BLOCK, 3 * BLOCK), BF16),
            jax.ShapeDtypeStruct((BLOCK, 6 * BLOCK), BF16),
            jax.ShapeDtypeStruct((n2, n2), F32),
        ),
        in_specs=[vmem, vmem, vmem, smem],
        out_specs=(hbm, hbm, vmem, vmem, vmem, vmem),
        scratch_shapes=[
            pltpu.VMEM((NR, HOP1, 128), F32),
            pltpu.VMEM((NR * HOP1, 128), F32),
            pltpu.VMEM((NC, 32, 128), F32),
            pltpu.VMEM((NC, 32, 128), F32),
            pltpu.VMEM((2, 2, SHARE, 128), F32),
            pltpu.VMEM((SHARE, 128), F32),
            pltpu.VMEM((steps, n2, STEP), F32),
            pltpu.VMEM((steps, n2, STEP), F32),
            pltpu.VMEM((steps, STEP, STEP), F32),
            pltpu.VMEM((n2, n2), F32),
            pltpu.VMEM((160, 8, 128), F32),
            pltpu.VMEM((n2, 3 * STEP), BF16),
            pltpu.VMEM((n2, 3 * STEP), BF16),
            dma((NR,)), dma((NR,)), dma((NC,)), dma((NC,)),
            dma((NC,)), dma((NC,)), dma((NR,)), dma((1,)), dma((NC,)), dma((NC,)),
            dma((2,)),
        ],
        compiler_params=pltpu.CompilerParams(
            collective_id=0, has_side_effects=True, vmem_limit_bytes=VMEM_LIMIT
        ),
        name="exchange",
    )(samples, position, slots, structure)


def halves(x):
    high = x.astype(BF16)
    return high, (x - high.astype(F32)).astype(BF16)


def three_left(x):
    high, rest = halves(x)
    return jnp.concatenate([high, rest, high], axis=1)


def three_right(x, axis=1):
    high, rest = halves(x)
    return jnp.concatenate([high, high, rest], axis=axis)


def inverse_factor(block, scratch):
    size = block.shape[0]
    eye = (iota((size, size), 0) == iota((size, size), 1)).astype(F32)
    both = jnp.concatenate([block, eye], axis=1)
    count = size // 8
    wide = (8, 2 * size)
    tiles = [both[8 * t : 8 * t + 8, :] for t in range(count)]
    sub = iota(wide, 0)
    out = []
    used = [0]

    def put(value):
        at = used[0]
        used[0] += 1
        scratch[at] = value
        return lambda k: jnp.broadcast_to(scratch[at, k : k + 1, :], wide)

    def spread(q, p):
        return [jnp.broadcast_to(tiles[q][:, 8 * p + j : 8 * p + j + 1], wide) for j in range(8)]

    ahead = spread(0, 0)
    for p in range(count):
        cols = {q: (ahead if q == p else spread(q, p)) for q in range(p, count)}
        ahead = spread(p + 1, p + 1) if p + 1 < count else None
        pivots = jnp.ones(wide, F32)
        for j in range(0, 8, 2):
            at1, at2, row = put(cols[p][j]), put(cols[p][j + 1]), put(tiles[p])
            a, b, c = at1(j), at1(j + 1), at2(j + 1)
            det = a * c - b * b
            inv1 = pltpu.reciprocal(a, approx=True)
            inv1 = inv1 * (2.0 - a * inv1)
            inv_det = pltpu.reciprocal(det, approx=True)
            inv2 = (a * inv_det) * (2.0 - det * inv_det)
            ratio = b * inv1
            pivots = jnp.where(sub == j, a, jnp.where(sub == j + 1, det * inv1, pivots))

            def scaled(x1, x2):
                return x1 * inv1, (x2 - ratio * x1) * inv2

            row1, row2 = scaled(row(j), row(j + 1))
            rest = [scaled(at1(k), at2(k)) for k in range(j + 2, 8)]
            for q in range(p, count):
                g1 = cols[q][j]
                g2 = cols[q][j + 1] - g1 * ratio
                if q == p:
                    g1 = jnp.where(sub > j, g1, 0.0)
                    g2 = jnp.where(sub > j + 1, g2, 0.0)
                for (u1, u2), k in zip(rest, range(j + 2, 8)):
                    cols[q][k] = (cols[q][k] - g1 * u1) - g2 * u2
                if q == p + 1:
                    next1, next2 = put(cols[q][j]), put(cols[q][j + 1])
                    for k in range(8):
                        u1, u2 = scaled(next1(k), next2(k))
                        ahead[k] = (ahead[k] - g1 * u1) - g2 * u2
                tiles[q] = (tiles[q] - g1 * row1) - g2 * row2
        scale = lax.rsqrt(pivots)
        scale = scale * (1.5 - 0.5 * pivots * scale * scale)
        out.append((tiles[p] * scale)[:, size:])
    return jnp.concatenate(out, axis=0)


def factor(cols_a, cols_l, inverses, x_ref, l_ref, scratch, below_l, below_r, after_first):
    steps, n, _ = cols_a.shape

    def step(start, i, block):
        base = start * STEP
        following = lax.rem(i + 1, steps)
        there = pl.ds(pl.multiple_of(following * STEP, STEP), STEP)
        for j in range(max(start, 1), steps):
            taken = mm(below_l[base:, :], below_r[j * STEP : (j + 1) * STEP], NT)
            cols_a[j, base:, :] = cols_a[j, base:, :] - taken
        left = three_left(cols_a[i, base:, :])
        inverse = inverse_factor(block, scratch)
        inverses[i] = inverse
        below = mm(left, three_right(inverse), NT)
        on = iota((n - base, STEP), 0) + base - i * STEP >= iota((n - base, STEP), 1)
        below = jnp.where(on, below, 0.0)
        cols_l[i, base:, :] = below
        below_l[base:, :] = three_left(below)
        below_r[base:, :] = three_right(below)
        return cols_a[following, there, :] - mm(below_l[there, :], below_r[there, :], NT)

    block = cols_a[0, 0:STEP, :]
    for start in range(0, steps, 2):
        block = lax.fori_loop(start, start + 2, functools.partial(step, start), block)
        if start == 0:
            after_first()
    for i in range(steps):
        l_ref[:, i * STEP : (i + 1) * STEP] = cols_l[i]
        x_ref[i * STEP : (i + 1) * STEP, i * STEP : (i + 1) * STEP] = inverses[i]
    size = STEP
    while size < n:
        for o in range(0, n, 2 * size):
            m, e = o + size, o + 2 * size
            part = mm(three_left(l_ref[m:e, o:m]), three_right(x_ref[o:m, o:m], 0))
            x_ref[m:e, o:m] = -mm(three_left(x_ref[m:e, m:e]), three_right(part, 0))
        size *= 2


def point_operands(packed, half):
    low = iota(packed.shape, 1) < FEAT
    turned = pltpu.roll(packed, FEAT, 1)
    x = jnp.where(jnp.logical_xor(low, half == 1), packed, turned) * (1.0 / RADIUS)
    norm = 0.5 * jnp.sum(x * x, axis=1, keepdims=True)

    def split(v):
        h = v.astype(BF16).astype(F32)
        m = (v - h).astype(BF16).astype(F32)
        return h, m, v - h - m

    h, m, l = split(x)
    nh, nm, nl = split(norm)
    lane = iota(packed.shape, 1)
    norms = jnp.where(lane % 3 == 0, nh, jnp.where(lane % 3 == 1, nm, nl))
    left_tail = jnp.where(lane < 3, norms, jnp.where(lane < 6, 1.0, 0.0))
    right_tail = jnp.where(lane < 3, 1.0, jnp.where(lane < 6, norms, 0.0))
    left = [h, jnp.where(low, h, m), jnp.where(low, m, l), left_tail]
    right = [
        -2.0 * jnp.where(low, h, m),
        -2.0 * jnp.where(low, l, h),
        -2.0 * jnp.where(low, m, h),
        right_tail,
    ]
    return (
        jnp.concatenate([g.astype(BF16) for g in left], axis=1),
        jnp.concatenate([g.astype(BF16) for g in right], axis=1),
    )


def kappa(squared, weight=1.0):
    x = jnp.maximum(squared, 1e-30)
    t = x * lax.rsqrt(x)
    s = jnp.maximum(1.0 - t, 0.0)
    s2 = s * s
    s4 = s2 * s2
    s8 = s4 * s4
    s16 = s8 * s8
    s32 = s16 * s16
    return (s32 * (s2 * s)) * (36.0 * weight - (35.0 * weight) * s)


def panel_kernel(
    slot_ref, structure_ref, row0_ref, rows_ref, cols_ref, diag_ref, x0_ref, x1_ref, l_ref, panel_ref, trailing_ref,
    order, sorted_cols, diag_rights, rights, cols3, left_now, left_next, rows3, wide, a3, a3_b, dist, prod, sem,
):
    k = pl.program_id(0)
    r = lax.axis_index("prow")
    c = lax.axis_index("pcol")
    chunk = 32

    def tile(j):
        return slice(BLOCK * j, BLOCK * (j + 1))

    def values(ident, start, stop, source, target):
        for b in range(2):
            w = structure_ref[ident, b].astype(F32)
            base = 3 * b
            for s in range(start, stop, chunk):
                h, l = halves(kappa(source[s : s + chunk, tile(b)], w))
                target[s : s + chunk, tile(base)] = h
                target[s : s + chunk, tile(base + 1)] = l
                target[s : s + chunk, tile(base + 2)] = h

    def first_product(source):
        return mm(source[:, : 3 * BLOCK], x0_ref[...], NT)

    def second_product(source):
        return mm(source[...], x1_ref[...], NT)

    @pl.when(k == 0)
    def _():
        def place(b, carry):
            order[slot_ref[b]] = b
            return carry

        lax.fori_loop(0, NBLK, place, 0)
        keys = [order[NC * m + c] for m in range(COLB)]
        keys = [jnp.where(key < 2, NBLK + key, key) for key in keys]
        for m in range(COLB):
            rank = sum(jnp.where(other < keys[m], 1, 0) for other in keys)
            sorted_cols[rank] = m
        for b in range(2):
            diag_rights[tile(b), :] = point_operands(diag_ref[...], b)[1]
        wides = [
            buffer.at[:, 2 * BLOCK * g : 2 * BLOCK * (g + 1)] for buffer in (dist, prod) for g in range(2)
        ]
        for j in range(COLB):
            m = sorted_cols[j]
            left, right = point_operands(cols_ref[m % 2], m // 2)
            rights[tile(j), :] = right
            wides[j][...] = mm(left, diag_rights[...], NT)
        left = point_operands(row0_ref[0, 0], 0)[0]
        left_next[...] = left
        buffers = (a3, a3_b)
        for j in range(COLB):
            values(order[NC * sorted_cols[j] + c], 0, BLOCK, wides[j], buffers[j % 2])
            source = buffers[j % 2]
            for b, value in enumerate((first_product(source), second_product(source))):
                high, rest = halves(value)
                cols3[tile(j), tile(3 * b)] = high
                cols3[tile(j), tile(3 * b + 1)] = high
                cols3[tile(j), tile(3 * b + 2)] = rest
        wide[...] = mm(left, diag_rights[...], NT)

    past = order[NR * jnp.maximum(k - 1, 0) + r]
    ident = order[NR * jnp.minimum(k, ROWB - 1) + r]
    col_ids = [order[NC * sorted_cols[j] + c] for j in range(COLB)]
    kept = sum(jnp.where((col >= 2) & (col <= past), 1, 0) for col in col_ids)
    kept = jnp.where(k == 0, 0, kept)

    def spot(j):
        return pl.ds(pl.multiple_of(sorted_cols[j] * BLOCK, BLOCK), BLOCK)

    def step(count, last):
        def trail(j):
            w = structure_ref[past, col_ids[j]].astype(F32)
            for s in range(0, BLOCK, chunk):
                value = kappa(dist[s : s + chunk, tile(j)], w) - prod[s : s + chunk, tile(j)]
                trailing_ref[s : s + chunk, spot(j)] = value

        if count:
            here = slice(0, BLOCK * count)
            dist[:, here] = mm(left_now[...], rights[here, :], NT)
        quarter = BLOCK // COLB
        for j in range(COLB):
            if j < count:
                prod[:, tile(j)] = mm(rows3[...], cols3[tile(j), :], NT)
            if not last:
                values(ident, quarter * j, quarter * (j + 1), wide, a3)
        if not last:
            c0 = first_product(a3)
        for j in range(count // 2):
            trail(j)
        if not last:
            c1 = second_product(a3)
            left = point_operands(rows_ref[0, 0], jnp.minimum(k + 1, ROWB - 1) // 4)[0]
            wide[...] = mm(left, diag_rights[...], NT)
        for j in range(count // 2, count):
            trail(j)
        for j in range(count, COLB):
            trailing_ref[:, spot(j)] = jnp.zeros((BLOCK, BLOCK), F32)
        if last:
            return
        left_now[...] = left_next[...]
        left_next[...] = left
        for b, value in enumerate((c0, c1)):
            high, rest = halves(value)
            panel_ref[:, tile(b)] = value
            rows3[:, tile(3 * b)] = high
            rows3[:, tile(3 * b + 1)] = rest
            rows3[:, tile(3 * b + 2)] = high

    for count in range(COLB + 1):

        @pl.when((kept == count) & (k < ROWB))
        def _():
            step(count, False)

        @pl.when((kept == count) & (k == ROWB))
        def _():
            step(count, True)

    @pl.when((ident < 2) & (k < ROWB))
    def _():
        source = pl.ds(pl.multiple_of(ident * BLOCK, BLOCK), BLOCK)
        copy = pltpu.make_async_copy(l_ref.at[source, :], panel_ref, sem)
        copy.start()
        copy.wait()

    for j in range(COLB):

        @pl.when((col_ids[j] == past) & (past >= 2))
        def _():
            eye = iota((BLOCK, BLOCK), 0) == iota((BLOCK, BLOCK), 1)
            trailing_ref[:, spot(j)] = trailing_ref[:, spot(j)] + jnp.where(eye, NUGGET, 0.0)


def panels_and_trailing(slots, structure, rows, cols, diag, x0, x1, lower):
    smem = pl.BlockSpec(memory_space=pltpu.SMEM)
    n2 = 2 * BLOCK
    n4 = COLB * BLOCK

    def row_block(k):
        k = jnp.minimum(k + 1, ROWB - 1)
        return (k % 4) // 2, k % 2, 0, 0

    return pl.pallas_call(
        panel_kernel,
        grid=(ROWB + 1,),
        out_shape=(
            jax.ShapeDtypeStruct((ROWB * BLOCK, n2), F32),
            jax.ShapeDtypeStruct((ROWB * BLOCK, n4), F32),
        ),
        in_specs=[
            smem,
            smem,
            pl.BlockSpec((1, 1, BLOCK, 128), lambda k: (0, 0, 0, 0)),
            pl.BlockSpec((1, 1, BLOCK, 128), row_block),
            pl.BlockSpec((2, BLOCK, 128), lambda k: (0, 0, 0)),
            pl.BlockSpec((BLOCK, 128), lambda k: (0, 0)),
            pl.BlockSpec((BLOCK, 3 * BLOCK), lambda k: (0, 0)),
            pl.BlockSpec((BLOCK, 6 * BLOCK), lambda k: (0, 0)),
            pl.BlockSpec(memory_space=pl.ANY),
        ],
        out_specs=(
            pl.BlockSpec((BLOCK, n2), lambda k: (jnp.minimum(k, ROWB - 1), 0)),
            pl.BlockSpec((BLOCK, n4), lambda k: (jnp.maximum(k - 1, 0), 0)),
        ),
        scratch_shapes=[
            pltpu.SMEM((NBLK,), I32),
            pltpu.SMEM((COLB,), I32),
            pltpu.VMEM((n2, n2), BF16),
            pltpu.VMEM((n4, n2), BF16),
            pltpu.VMEM((n4, 3 * n2), BF16),
            pltpu.VMEM((BLOCK, n2), BF16),
            pltpu.VMEM((BLOCK, n2), BF16),
            pltpu.VMEM((BLOCK, 3 * n2), BF16),
            pltpu.VMEM((BLOCK, n2), F32),
            pltpu.VMEM((BLOCK, 3 * n2), BF16),
            pltpu.VMEM((BLOCK, 3 * n2), BF16),
            pltpu.VMEM((BLOCK, n4), F32),
            pltpu.VMEM((BLOCK, n4), F32),
            pltpu.SemaphoreType.DMA,
        ],
        compiler_params=pltpu.CompilerParams(vmem_limit_bytes=VMEM_LIMIT),
        name="panels",
    )(slots, structure, rows, rows, cols, diag, x0, x1, lower)


def shards(samples, position, slot_of_block, structure):
    parts = exchange(
        samples.T, position.reshape(1, SRC), slot_of_block.reshape(1, NBLK), structure
    )
    return panels_and_trailing(slot_of_block, structure, *parts)


def solution(mesh):
    in_specs = (P(("prow", "pcol"), None), P(("prow", "pcol")), P(), P())
    out_specs = (P("prow", None), P("prow", "pcol"))
    return jax.shard_map(shards, mesh=mesh, in_specs=in_specs, out_specs=out_specs, check_vma=False)
```

time: 792 us -> 70.6 us (0.09)
  waiting for transfers between devices: 474 us -> 0 us
  other arithmetic: 132 us -> 0 us
  Pallas kernels: 0 us -> 68.6 us
  matrix products: 57.6 us -> 0 us
  local copies, waits for them, and re-layouts: 55.4 us -> 0 us
  blocking collectives: 22.3 us -> 0 us
  between operations: 22.7 us -> 0.8 us
  starting transfers between devices: 20.7 us -> 0 us
    psum x7 -> x0, waiting for transfers between devices: 467 us -> none  [spread(): return lax.psum(block, axis)]
    another operation x19 -> x0, other arithmetic: 110 us -> none  [the longest x13 69.2 us: inverse_lower(): lower_factor = jnp.linalg.cholesky(matrix)]
    pallas_call x0 -> x2, Pallas kernels: none -> 68.6 us  [the longest x1 47.5 us: exchange(): pl.pallas_call(exchange_kernel, out_shape=(jax.ShapeDtypeStruct((2, 2, BL...]
    dot_general x7 -> x0, matrix products: 54.6 us -> none  [the longest x1 16.1 us: kernel_values(): jnp.einsum('af,bf->ab', left_rows, right_rows, precision=HIGHEST)]
    unnamed x13 -> x0, local copies, waits for them, and re-layouts: 26.4 us -> none
    all_gather x1 -> x0, blocking collectives: 22.3 us -> none  [shards(): lax.all_gather(local_rows.reshape(row_blocks, row_share * features), 'pco...]
    all_to_all x2 -> x0, starting transfers between devices: 20.2 us -> none  [the longest x1 10.4 us: shards(): lax.all_to_all(send_places.reshape(devices, capacity), ('prow', 'pcol'),...]
    reshape x3 -> x0, local copies, waits for them, and re-layouts: 11.3 us -> none  [the longest x1 11.1 us: shards(): values.reshape(row_blocks, BLOCK, col_blocks, BLOCK)]
  transfers between devices with their start and end apart: 9 -> 0, of which waited for: 9 -> 0; matrix products, arithmetic and copies ran while one was open for 3% -> 0% of each run, Pallas kernels for 0% -> 0%
where the time goes in v1:
time: 70.6 us; the launch traced here: 69.4 us
  Pallas kernels  68.6 us (97%)
  between operations  0.8 us (1%)
    pallas_call x1, Pallas kernels, exchange(): pl.pallas_call(exchange_kernel, out_shape=(jax.ShapeDtypeStruct((2, 2, BL...  47.5 us
    pallas_call x1, Pallas kernels, panels_and_trailing(): pl.pallas_call(panel_kernel, grid=(ROWB + 1,), out_shape=(jax.ShapeDtypeS...  21.1 us

profile of v1, /device:TPU:8, one launch (start us, length us, event | category | flops | bytes accessed | tf_op | source)
XLA Modules:
  0.0 69.4 jit_solution(11645498053293118645)
XLA Ops:
  0.6 47.5 %exchange.1 = (f32[2,2,256,128]{3,2,1,0:T(8,128)}, f32[2,256,128]{2,1,0:T(8,128)}, f32[256,128]{1,0:T(8,128)}, bf16[256,768]{1,0:T(8,128)(2,1)}, bf16[256,1536]{1,0:T(8,128)(2,1)}, /*index=5*/f32[512,512]{1,0:T(8,128)}) custom-call(f32[64,128]{1,0:T(8,128)} %bitcast.3, s32[1,128]{1,0:T(1,128)} %bitcast.5, s32[1,64]{1,0:T(1,128)} %bitcast.4, ...), custom_call_target="tpu_custom_call" | custom-call | tf_op jit(solution)/shard_map/exchange/pallas_call | solution.py:276
  48.2 21.1 %panels.1 = (f32[2048,512]{1,0:T(8,128)}, f32[2048,1024]{1,0:T(8,128)}) custom-call(s32[64]{0:T(128)} %slot_ref.1, s32[64,64]{1,0:T(8,128)} %structure_ref.3, f32[2,2,256,128]{3,2,1,0:T(8,128)} %get-tuple-element.8.row0_ref.rows_ref, f32[2,2,256,128]{3,2,1,0:T(8,128)} %get-tuple-element.8.row0_ref.rows_ref, f32[2,256,128]{2,1,0:T(8,128)} %get-tuple-element.9.cols_ref, ...), custom_call_target="tpu_custom_call" | custom-call | tf_op jit(solution)/shard_map/panels/pallas_call | solution.py:614

commit v2 on v1

--- a/solution.py
+++ b/solution.py
@@ -48,8 +48,8 @@
 
 def exchange_kernel(
     samples_ref, position_ref, slot_ref, structure_ref,
-    rows_ref, cols_ref, diag_ref, x0_ref, x1_ref, l_ref,
-    buf1, recv1, buf2, recv2, chunk, dshare, cols_a, cols_l, inverses, whole, scratch, below_l, below_r,
+    rows_ref, cols_ref, diag_ref, x0_out, x1_out, l_out,
+    buf1, recv1, buf2, recv2, chunk, dshare, cols_a, cols_l, inverses, whole, scratch, below_l, below_r, l_ref, x0_ref, x1_ref,
     s1, r1, s2, r2, s4, r4, s5, r5, s6, r6, own,
 ):
     r = lax.axis_index("prow")
@@ -242,15 +242,34 @@
                 col_copy(d).start()
             own_cols.start()
 
-    factor(cols_a, cols_l, inverses, whole, l_ref, scratch, below_l, below_r, pass_columns)
-    high, rest = halves(whole[...])
-    for x_ref, top, count in ((x0_ref, 0, 1), (x1_ref, BLOCK, 2)):
-        for b in range(count):
-            spot = (slice(top, top + BLOCK), slice(BLOCK * b, BLOCK * (b + 1)))
-            base = 3 * BLOCK * b
-            x_ref[:, base : base + BLOCK] = high[spot]
-            x_ref[:, base + BLOCK : base + 2 * BLOCK] = high[spot]
-            x_ref[:, base + 2 * BLOCK : base + 3 * BLOCK] = rest[spot]
+    def keep(x_ref, at, top, b):
+        high, rest = halves(whole[top : top + BLOCK, BLOCK * b : BLOCK * (b + 1)])
+        x_ref[:, at : at + BLOCK] = high
+        x_ref[:, at + BLOCK : at + 2 * BLOCK] = high
+        x_ref[:, at + 2 * BLOCK : at + 3 * BLOCK] = rest
+
+    wide = 3 * BLOCK
+    leaving = [
+        pltpu.make_async_copy(l_ref, l_out, own.at[2]),
+        pltpu.make_async_copy(x0_ref, x0_out, own.at[3]),
+        pltpu.make_async_copy(
+            x1_ref.at[:, pl.ds(wide, wide)], x1_out.at[:, pl.ds(wide, wide)], own.at[4]
+        ),
+        pltpu.make_async_copy(x1_ref.at[:, pl.ds(0, wide)], x1_out.at[:, pl.ds(0, wide)], own.at[5]),
+    ]
+
+    def before_last():
+        keep(x0_ref, 0, 0, 0)
+        keep(x1_ref, wide, BLOCK, 1)
+        leaving[1].start()
+        leaving[2].start()
+
+    factor(
+        cols_a, cols_l, inverses, whole, l_ref, scratch, below_l, below_r,
+        pass_columns, leaving[0].start, before_last,
+    )
+    keep(x1_ref, 0, BLOCK, 0)
+    leaving[3].start()
 
     @pl.when(source_row == r)
     def _():
@@ -264,6 +283,8 @@
 
     for copy in row_copies + diag_copies:
         copy.wait_send()
+    for copy in leaving:
+        copy.wait()
 
 
 def exchange(samples, position, slots, structure):
@@ -284,7 +305,7 @@
             jax.ShapeDtypeStruct((n2, n2), F32),
         ),
         in_specs=[vmem, vmem, vmem, smem],
-        out_specs=(hbm, hbm, vmem, vmem, vmem, vmem),
+        out_specs=(hbm, hbm, vmem, hbm, hbm, hbm),
         scratch_shapes=[
             pltpu.VMEM((NR, HOP1, 128), F32),
             pltpu.VMEM((NR * HOP1, 128), F32),
@@ -299,9 +320,12 @@
             pltpu.VMEM((160, 8, 128), F32),
             pltpu.VMEM((n2, 3 * STEP), BF16),
             pltpu.VMEM((n2, 3 * STEP), BF16),
+            pltpu.VMEM((n2, n2), F32),
+            pltpu.VMEM((BLOCK, 3 * BLOCK), BF16),
+            pltpu.VMEM((BLOCK, 6 * BLOCK), BF16),
             dma((NR,)), dma((NR,)), dma((NC,)), dma((NC,)),
             dma((NC,)), dma((NC,)), dma((NR,)), dma((1,)), dma((NC,)), dma((NC,)),
-            dma((2,)),
+            dma((6,)),
         ],
         compiler_params=pltpu.CompilerParams(
             collective_id=0, has_side_effects=True, vmem_limit_bytes=VMEM_LIMIT
@@ -386,7 +410,9 @@
     return jnp.concatenate(out, axis=0)
 
 
-def factor(cols_a, cols_l, inverses, x_ref, l_ref, scratch, below_l, below_r, after_first):
+def factor(
+    cols_a, cols_l, inverses, x_ref, l_ref, scratch, below_l, below_r, after_first, after_lower, before_last
+):
     steps, n, _ = cols_a.shape
 
     def step(start, i, block):
@@ -415,8 +441,11 @@
     for i in range(steps):
         l_ref[:, i * STEP : (i + 1) * STEP] = cols_l[i]
         x_ref[i * STEP : (i + 1) * STEP, i * STEP : (i + 1) * STEP] = inverses[i]
+    after_lower()
     size = STEP
     while size < n:
+        if 2 * size == n:
+            before_last()
         for o in range(0, n, 2 * size):
             m, e = o + size, o + 2 * size
             part = mm(three_left(l_ref[m:e, o:m]), three_right(x_ref[o:m, o:m], 0))

time: 70.6 us -> 73 us (1.034); the launches traced: 69.4 us -> 72.7 us
  Pallas kernels: 68.6 us -> 71.9 us
    pallas_call x1, Pallas kernels: 21.1 us -> 23.9 us  [panels_and_trailing(): pl.pallas_call(panel_kernel, grid=(ROWB + 1,), out_shape=(jax.ShapeDtypeS...]
where the time goes in v2:
time: 73 us; the launch traced here: 72.7 us
  Pallas kernels  71.9 us (98%)
  between operations  0.8 us (1%)
    pallas_call x1, Pallas kernels, exchange(): pl.pallas_call(exchange_kernel, out_shape=(jax.ShapeDtypeStruct((2, 2, BL...  48 us
    pallas_call x1, Pallas kernels, panels_and_trailing(): pl.pallas_call(panel_kernel, grid=(ROWB + 1,), out_shape=(jax.ShapeDtypeS...  23.9 us

profile of v2, /device:TPU:8, one launch (start us, length us, event | category | flops | bytes accessed | tf_op | source)
XLA Modules:
  0.0 72.7 jit_solution(14131872164216171924)
XLA Ops:
  0.6 48.0 %exchange.1 = (f32[2,2,256,128]{3,2,1,0:T(8,128)}, f32[2,256,128]{2,1,0:T(8,128)}, f32[256,128]{1,0:T(8,128)}, bf16[256,768]{1,0:T(8,128)(2,1)}, bf16[256,1536]{1,0:T(8,128)(2,1)}, /*index=5*/f32[512,512]{1,0:T(8,128)}) custom-call(f32[64,128]{1,0:T(8,128)} %bitcast.3, s32[1,128]{1,0:T(1,128)} %bitcast.5, s32[1,64]{1,0:T(1,128)} %bitcast.4, ...), custom_call_target="tpu_custom_call" | custom-call | tf_op jit(solution)/shard_map/exchange/pallas_call | solution.py:297
  48.7 23.9 %panels.1 = (f32[2048,512]{1,0:T(8,128)}, f32[2048,1024]{1,0:T(8,128)}) custom-call(s32[64]{0:T(128)} %slot_ref.1, s32[64,64]{1,0:T(8,128)} %structure_ref.3, f32[2,2,256,128]{3,2,1,0:T(8,128)} %get-tuple-element.8.row0_ref.rows_ref, f32[2,2,256,128]{3,2,1,0:T(8,128)} %get-tuple-element.8.row0_ref.rows_ref, f32[2,256,128]{2,1,0:T(8,128)} %get-tuple-element.9.cols_ref, ...), custom_call_target="tpu_custom_call" | custom-call | tf_op jit(solution)/shard_map/panels/pallas_call | solution.py:643
